TPU v7x, 128 devices: a whole 4x4x4 slice. The times are simulated.
128 devices in a mesh: seq: 8 (over x, y_lo), dp: 16 (over y_hi, z, core).
Axes of the slice: x: 4, y: 4 (y_hi: 2, y_lo: 2; y = y_hi * 2 + y_lo), z: 4, core: 2. Of those that a mesh axis runs over, the one named last changes fastest.
Arguments:
- tokens: bfloat16 [16, 8192, 1024], P('dp', 'seq'), may hold values from -6 to 6
- w_qkv: bfloat16 [1024, 3072], replicated
- offsets: int32 [16, 16], P('dp'), may hold values from 0 to 7, as said below
- d_attended: bfloat16 [16, 8192, 1024], P('dp', 'seq'), may hold values from -6 to 6
Outputs:
- attended: bfloat16 [16, 8192, 1024], P('dp', 'seq')
- d_tokens: bfloat16 [16, 8192, 1024], P('dp', 'seq')
- d_weights: float32 [1024, 3072], P('seq')
Inputs may be any that keep to these rules, and one draw needn't show every extreme that they name: offsets[n, h] is below min(2 ** (h // 4), 8), the span of head h's group.
All inputs are finite; a program needn't handle non-finite values.
Results may differ from a plain program's by a relative error of at most 0.039.
The roundings to bfloat16 on the way count: a program that leaves them out, or rounds other values in their place, can miss the bound.
Values may be sent and summed in bfloat16 or wider, within the bound.
No kernel may reach another device: no remote copies, remote signals or barrier semaphores. Data moves between devices by JAX's collectives and lax.ppermute only.
A program may use at most 128 MiB of HBM per device.

v0:
```python
import jax
import jax.numpy as jnp
from jax import lax
from jax.sharding import PartitionSpec as P

HEADS = 16
HEAD_DIM = 64
BLK = 128


def partner_2(block, axis, distance):
    count = lax.axis_size(axis)
    route = []
    for low in range(count):
        high = low | 1 << distance
        if high != low and high < count:
            route += [(low, high), (high, low)]
    return lax.ppermute(block, axis, route)


def product(form, left, right):
    return jnp.einsum(form, left, right, preferred_element_type=jnp.float32)


def select(row_block, chosen):
    span = chosen.shape[0]
    row_total, columns = row_block.shape
    blocks = row_block.reshape(row_total // (BLK * span), span, BLK, columns)
    picked = jnp.sum(
        jnp.where(chosen[None, :, None, :], blocks, jnp.zeros((), row_block.dtype)), axis=1
    )
    return picked.reshape(row_total // span, columns)


def spread(compact, chosen):
    columns = compact.shape[1]
    blocks = compact.reshape(-1, 1, BLK, columns)
    full = jnp.where(chosen[None, :, None, :], blocks, jnp.zeros((), compact.dtype))
    return full.reshape(-1, columns)


def scores_of(query, keys):
    row_total, columns = query.shape
    heads_here = columns // HEAD_DIM
    query3 = query.reshape(row_total, heads_here, HEAD_DIM)
    keys3 = keys.reshape(keys.shape[0], heads_here, HEAD_DIM)
    return product("qhd,khd->hqk", query3, keys3) * 0.125


def attend(query, keys, values):
    row_total, columns = query.shape
    heads_here = columns // HEAD_DIM
    scores = scores_of(query, keys)
    highest = jnp.max(scores, axis=2, keepdims=True)
    row_sums = jnp.sum(jnp.exp(scores - highest), axis=2, keepdims=True)
    log_total = highest + jnp.log(row_sums)
    attention_b = jnp.exp(scores - log_total).astype(jnp.bfloat16)
    values3 = values.reshape(values.shape[0], heads_here, HEAD_DIM)
    output = product("hqk,khd->qhd", attention_b, values3)
    return (output.reshape(row_total, columns).astype(jnp.bfloat16), log_total)


def attend_back(query, keys, values, log_total, output, incoming):
    row_total, columns = query.shape
    heads_here = columns // HEAD_DIM
    scores = scores_of(query, keys)
    attention = jnp.exp(scores - log_total)
    attention_b = attention.astype(jnp.bfloat16)
    query3 = query.reshape(row_total, heads_here, HEAD_DIM)
    keys3 = keys.reshape(keys.shape[0], heads_here, HEAD_DIM)
    values3 = values.reshape(values.shape[0], heads_here, HEAD_DIM)
    incoming3 = incoming.reshape(row_total, heads_here, HEAD_DIM)
    output3 = output.reshape(row_total, heads_here, HEAD_DIM)
    grad_prob = product("qhd,khd->hqk", incoming3, values3)
    delta = jnp.sum(incoming3.astype(jnp.float32) * output3.astype(jnp.float32), axis=2)
    grad_score = (attention * (grad_prob - jnp.transpose(delta)[:, :, None])).astype(jnp.bfloat16)
    grad_query = product("hqk,khd->qhd", grad_score, keys3) * 0.125
    grad_keys = product("hqk,qhd->khd", grad_score, query3) * 0.125
    grad_values = product("hqk,qhd->khd", attention_b, incoming3)
    return (
        grad_query.reshape(row_total, columns),
        grad_keys.reshape(-1, columns),
        grad_values.reshape(-1, columns),
    )


def collect(pieces, spans):
    own_index = lax.axis_index("seq")
    blocks = list(pieces)
    level_count = max(spans).bit_length() - 1
    for bit_level in range(level_count):
        active = [group for group in range(len(blocks)) if spans[group] > 2**bit_level]
        lengths = [blocks[group].shape[0] for group in active]
        joined = jnp.concatenate([blocks[group] for group in active], axis=0)
        received = partner_2(joined, "seq", bit_level)
        upper_half = own_index // 2**bit_level % 2 == 1
        position = 0
        for group, length in zip(active, lengths):
            partner = received[position : position + length]
            position = position + length
            blocks[group] = jnp.where(
                upper_half,
                jnp.concatenate([partner, blocks[group]], axis=0),
                jnp.concatenate([blocks[group], partner], axis=0),
            )
    return blocks


def send_back(grads, spans):
    own_index = lax.axis_index("seq")
    blocks = list(grads)
    level_count = max(spans).bit_length() - 1
    for bit_level in reversed(range(level_count)):
        active = [group for group in range(len(blocks)) if spans[group] > 2**bit_level]
        upper_half = own_index // 2**bit_level % 2 == 1
        staying, leaving = ([], [])
        for group in active:
            halfway = blocks[group].shape[0] // 2
            lower_rows = blocks[group][:halfway]
            higher_rows = blocks[group][halfway:]
            staying.append(jnp.where(upper_half, higher_rows, lower_rows))
            leaving.append(jnp.where(upper_half, lower_rows, higher_rows))
        received = partner_2(jnp.concatenate(leaving, axis=0), "seq", bit_level)
        position = 0
        for group, kept_rows in zip(active, staying):
            length = kept_rows.shape[0]
            blocks[group] = kept_rows + received[position : position + length]
            position = position + length
    return blocks


def per_device(tokens, w_qkv, offsets, d_attended):
    inputs = tokens[0]
    incoming = d_attended[0]
    offset_row = offsets[0]
    seq_count = lax.axis_size("seq")
    own_index = lax.axis_index("seq")
    row_total, model_width = inputs.shape
    per_group = HEADS // 4
    columns = per_group * HEAD_DIM
    qkv = jnp.dot(inputs, w_qkv, preferred_element_type=jnp.float32).astype(jnp.bfloat16)
    spans = [min(2**group, seq_count) for group in range(4)]
    chosen_list, queries, pair_pieces = ([], [], [])
    for group in range(4):
        first_col = group * columns
        column_offsets = jnp.repeat(
            offset_row[group * per_group : (group + 1) * per_group], HEAD_DIM
        )
        chosen = jnp.arange(spans[group])[:, None] == column_offsets[None, :]
        chosen_list.append(chosen)
        queries.append(select(qkv[:, first_col : first_col + columns], chosen))
        key_rows = select(
            qkv[:, model_width + first_col : model_width + first_col + columns], chosen
        )
        value_rows = select(
            qkv[:, 2 * model_width + first_col : 2 * model_width + first_col + columns], chosen
        )
        pair_pieces.append(jnp.concatenate([key_rows, value_rows], axis=1))
    gathered = collect(pair_pieces, spans)
    outputs, log_totals, positions_list = ([], [], [])
    for group in range(4):
        compact_rows = row_total // spans[group]
        positions = own_index % spans[group] * compact_rows + jnp.arange(compact_rows)
        positions_list.append(positions)
        result, log_total = attend(
            queries[group], gathered[group][:, :columns], gathered[group][:, columns:]
        )
        outputs.append(result)
        log_totals.append(log_total)
    attended = jnp.concatenate(
        [spread(outputs[group], chosen_list[group]) for group in range(4)], axis=1
    )
    grad_q, pair_grads = ([], [])
    for group in range(4):
        first_col = group * columns
        grads_in = select(incoming[:, first_col : first_col + columns], chosen_list[group])
        keys_all = gathered[group][:, :columns]
        values_all = gathered[group][:, columns:]
        back_q, back_k, back_v = attend_back(
            queries[group], keys_all, values_all, log_totals[group], outputs[group], grads_in
        )
        grad_q.append(back_q)
        pair_grads.append(jnp.concatenate([back_k, back_v], axis=1))
    owned = send_back(pair_grads, spans)
    query_part = [spread(grad_q[group], chosen_list[group]) for group in range(4)]
    key_part = [spread(owned[group][:, :columns], chosen_list[group]) for group in range(4)]
    value_part = [spread(owned[group][:, columns:], chosen_list[group]) for group in range(4)]
    d_qkv = jnp.concatenate(query_part + key_part + value_part, axis=1).astype(jnp.bfloat16)
    d_inputs = lax.dot_general(
        d_qkv, w_qkv, (((1,), (1,)), ((), ())), preferred_element_type=jnp.float32
    ).astype(jnp.bfloat16)
    partial_rows = lax.psum_scatter(
        lax.dot_general(
            inputs, d_qkv, (((0,), (0,)), ((), ())), preferred_element_type=jnp.float32
        ),
        ("seq", "dp"),
        scatter_dimension=0,
        tiled=True,
    )
    d_weights = lax.all_gather(partial_rows, "dp", axis=0, tiled=True)
    return (attended[None], d_inputs[None], d_weights)


def solution(mesh):
    placed = (P("dp", "seq", None), P(), P("dp", None), P("dp", "seq", None))
    return jax.shard_map(
        per_device,
        mesh=mesh,
        in_specs=placed,
        out_specs=(P("dp", "seq", None), P("dp", "seq", None), P("seq", None)),
        check_vma=False,
    )
```

profile of v0, /device:TPU:1, one launch (start us, length us, event | category | flops | bytes accessed | tf_op | source)
XLA Modules:
  0.0 1028.9 jit_solution(2086188496058811215)
XLA Ops:
  8.6 2.5 fusion.43
  11.1 9.6 convolution_convert_fusion
  27.5 2.3 collective-permute-start
  31.2 2.0 copy.100
  34.8 1.7 copy.123
  38.8 1.7 copy.110
  44.4 2.0 copy.121
  46.4 1.8 reshape_reshape.22
  49.1 1.8 reshape_reshape.18
  50.8 9.2 multiply_reduce_fusion
  60.1 8.5 exponential_reduce_fusion
  68.6 10.0 multiply_reduce_fusion.4
  79.5 6.7 multiply_convert_fusion
  86.3 3.9 fusion.7
  91.1 1.7 maximum_select_fusion.5
  100.0 2.1 pad_maximum_fusion.5
  104.7 1.8 exponential_reduce_fusion.1
  109.2 6.5 multiply_reduce_fusion.5
  115.8 4.8 collective-permute-done.1
  126.6 3.0 collective-permute-start.2
  129.6 1.8 multiply_reduce_fusion.2
  132.3 2.2 multiply_reduce_fusion.6
  134.5 5.6 collective-permute-done.2
  148.0 1.7 multiply_convert_fusion.3
  151.0 2.5 copy.133
  153.5 2.5 copy.134
  156.1 2.7 broadcast_select_fusion.4
  158.8 2.7 collective-permute-start.3
  161.5 3.6 multiply_convert_fusion.2
  167.8 2.6 copy.131
  170.4 4.1 fusion.22
  174.5 2.5 copy.132
  177.0 1.7 broadcast_select_fusion.5
  178.8 3.7 collective-permute-done.3
  182.4 2.1 select_add_fusion
  187.5 4.8 multiply_convert_fusion.1
  192.2 1.9 copy-done.4
  194.2 1.8 convolution_multiply_fusion.4
  196.0 2.6 copy.129
  198.6 6.0 fusion.16
  204.6 2.6 copy.130
  207.1 1.8 broadcast_select_fusion.7
  209.0 9.8 collective-permute-done.4
  220.3 2.0 slice_add_fusion.1
  224.9 2.4 convolution_multiply_fusion.3
  227.5 2.1 copy.136
  229.6 2.0 copy.120
  231.6 7.1 convolution_multiply_fusion.2
  238.7 2.0 copy.128
  240.8 2.1 copy.104
  242.8 2.1 fusion.19
  246.8 4.5 fusion.6
  251.3 1.7 broadcast_in_dim.382
  253.0 1.8 copy.122
  256.5 3.2 fusion.11
  261.3 1.7 copy.124
  264.5 2.2 convolution_multiply_fusion.7
  285.5 12.7 %convolution_bitcast_fusion = f32[1024,3072]{0,1:T(8,128)} fusion(bf16[1024,3072]{1,0:T(8,128)(2,1)} %constant_dynamic-update-slice_fusion, bf16[1,1024,1024]{2,1,0:T(8,128)(2,1)S(1)} %copy-done), kind=kOutput, calls=%fused_computation.10 | convolution fusion | flops 6442450944 | bytes 20971520 | tf_op jit(solution)/shard_map/dot_general | solution.py:193
  298.3 12.6 %copy.143 = f32[1024,3072]{1,0:T(8,128)} copy(f32[1024,3072]{0,1:T(8,128)} %convolution_bitcast_fusion) | data formatting | bytes 25165824
  310.9 657.8 %reduce-scatter.4.cloned.1.call-done = f32[8,3072]{1,0:T(8,128)} async-done(((f32[1024,3072]{1,0:T(8,128)}), f32[8,3072]{1,0:T(8,128)}) %reduce-scatter.4.cloned.1.call-update) | async-done | bytes 98320 | tf_op jit(solution)/shard_map/reduce_scatter | solution.py:192
  968.8 2.8 maximum_bitcast_fusion
  971.6 11.6 %convert_bitcast_fusion = bf16[1,1024,1024]{2,1,0:T(8,128)(2,1)} fusion(bf16[1024,3072]{1,0:T(8,128)(2,1)} %constant_dynamic-update-slice_fusion, bf16[1024,3072]{1,0:T(8,128)(2,1)} %param.5), kind=kOutput, calls=%fused_computation.26 | convolution fusion | flops 6443499520 | bytes 14680064 | tf_op jit(solution)/shard_map/dot_general | solution.py:189
  983.2 35.7 %all-gather.2.cloned.1.call-done = f32[128,3072]{1,0:T(8,128)} async-done(((f32[8,3072]{1,0:T(8,128)}), f32[128,3072]{1,0:T(8,128)}) %all-gather.2.cloned.1.call-update) | async-done | bytes 1572880 | tf_op jit(solution)/shard_map/all_gather | solution.py:200
  1018.9 2.7 copy.157
  (211 shorter events, 83.9 us)
Async XLA Ops:
  7.2 3.9 copy-start
  7.2 961.6 %reduce-scatter.4.cloned.1.call-start = ((), (), s32[]{:S(2)}) async-start(), calls=%async_computation.2 | async-start | bytes 12681216 | tf_op jit(solution)/shard_map/reduce_scatter | solution.py:192
  8.3 16.2 %copy-start.51 = (pred[2,256]{1,0:T(4,128)(4,1)}, pred[2,256]{1,0:T(4,128)(4,1)S(1)}, u32[]{:S(2)}) copy-start(pred[2,256]{1,0:T(4,128)(4,1)S(1)} %iota_compare_fusion.2) | copy-start | bytes 1540
  8.5 13.8 %copy-start.47 = (pred[8,256]{1,0:T(8,128)(4,1)}, pred[8,256]{1,0:T(8,128)(4,1)S(1)}, u32[]{:S(2)}) copy-start(pred[8,256]{1,0:T(8,128)(4,1)S(1)} %iota_compare_fusion) | copy-start | bytes 6148
  8.6 14.6 %copy-start.49 = (pred[4,256]{1,0:T(4,128)(4,1)}, pred[4,256]{1,0:T(4,128)(4,1)S(1)}, u32[]{:S(2)}) copy-start(pred[4,256]{1,0:T(4,128)(4,1)S(1)} %iota_compare_fusion.1) | copy-start | bytes 3076
  23.3 6.6 copy-start.39
  23.3 6.6 copy-start.40
  23.3 6.6 copy-start.53
  24.4 5.4 copy-start.33
  24.4 5.4 copy-start.34
  25.8 0.7 copy-start.25
  25.8 1.7 copy-start.26
  27.5 62.7 %collective-permute-start = (bf16[896,512]{1,0:T(8,128)(2,1)}, bf16[896,512]{1,0:T(8,128)(2,1)}, u32[]{:S(2)}, u32[]{:S(2)}) collective-permute-start(bf16[896,512]{1,0:T(8,128)(2,1)} %maximum_maximum_fusion), channel_id=1, source_target_pairs={{0,16},{16,0},{32,48},{48,32},{64,80},{80,64},{96,112},{112,96},{1... | collective-permute-start | bytes 2752520 | tf_op jit(solution)/shard_map/ppermute | solution.py:18
  44.4 15.7 %copy-start.11 = (bf16[1024,256]{0,1:T(8,128)(2,1)}, bf16[1024,256]{0,1:T(8,128)(2,1)S(1)}, u32[]{:S(2)}) copy-start(bf16[1024,256]{0,1:T(8,128)(2,1)S(1)} %copy.101) | copy-start | bytes 1572868
  68.6 10.9 %copy-start.1 = (f32[4,1024,1024]{1,2,0:T(8,128)S(1)}, f32[4,1024,1024]{1,2,0:T(8,128)}, u32[]{:S(2)}) copy-start(f32[4,1024,1024]{1,2,0:T(8,128)} %get-tuple-element.79) | copy-start | bytes 50331652
  68.6 10.9 %copy-start.21 = (bf16[1024,256]{0,1:T(8,128)(2,1)S(1)}, bf16[1024,256]{0,1:T(8,128)(2,1)}, u32[]{:S(2)}) copy-start(bf16[1024,256]{0,1:T(8,128)(2,1)} %copy.100) | copy-start | bytes 1572868
  95.0 8.3 copy-start.23
  100.0 4.7 copy-start.20
  102.1 18.4 %collective-permute-start.1 = (bf16[768,512]{1,0:T(8,128)(2,1)}, bf16[768,512]{1,0:T(8,128)(2,1)}, u32[]{:S(2)}, u32[]{:S(2)}) collective-permute-start(bf16[768,512]{1,0:T(8,128)(2,1)} %pad_maximum_fusion.5), channel_id=1, source_target_pairs={{0,32},{32,0},{16,48},{48,16},{64,96},{96,64},{80,112},{112,80},{1... | collective-permute-start | bytes 2359304 | tf_op jit(solution)/shard_map/ppermute | solution.py:18
  104.7 3.2 copy-start.2
  104.7 4.5 copy-start.22
  109.2 6.6 copy-start.13
  109.2 12.2 %copy-start.27 = (bf16[256,512]{1,0:T(8,128)(2,1)S(1)}, bf16[256,512]{1,0:T(8,128)(2,1)}, u32[]{:S(2)}) copy-start(bf16[256,512]{1,0:T(8,128)(2,1)} %maximum_select_fusion.5) | copy-start | bytes 786436
  125.1 7.2 copy-start.19
  126.6 5.7 copy-start.17
  126.6 13.5 %collective-permute-start.2 = (bf16[512,512]{1,0:T(8,128)(2,1)}, bf16[512,512]{1,0:T(8,128)(2,1)S(1)}, u32[]{:S(2)}, u32[]{:S(2)}) collective-permute-start(bf16[512,512]{1,0:T(8,128)(2,1)} %maximum_select_fusion.4), channel_id=1, source_target_pairs={{0,64},{64,0},{16,80},{80,16},{32,96},{96,32},{48,112},{112,48},{1... | collective-permute-start | bytes 1572872 | tf_op jit(solution)/shard_map/ppermute | solution.py:18
  129.6 2.7 copy-start.28
  131.3 3.2 copy-start.3
  131.3 8.8 copy-start.31
  141.6 4.8 copy-start.16
  143.1 4.9 copy-start.18
  143.1 2.1 copy-start.36
  145.2 4.5 copy-start.41
  158.8 7.6 copy-start.35
  158.8 23.7 %collective-permute-start.3 = (f32[512,512]{1,0:T(8,128)}, f32[512,512]{1,0:T(8,128)}, u32[]{:S(2)}, u32[]{:S(2)}) collective-permute-start(f32[512,512]{1,0:T(8,128)} %broadcast_select_fusion.4), channel_id=1, source_target_pairs={{0,64},{64,0},{16,80},{80,16},{32,96},{96,32},{48,112},{112,48},{1... | collective-permute-start | bytes 3145736 | tf_op jit(solution)/shard_map/ppermute | solution.py:18
  165.0 1.3 copy-start.5
  178.7 8.7 copy-start.14
  178.7 8.7 copy-start.46
  184.6 2.9 copy-start.8
  186.1 32.7 %collective-permute-start.4 = (f32[768,512]{1,0:T(8,128)}, f32[768,512]{1,0:T(8,128)}, u32[]{:S(2)}, u32[]{:S(2)}) collective-permute-start(f32[768,512]{1,0:T(8,128)} %pad_maximum_fusion.1), channel_id=1, source_target_pairs={{0,32},{32,0},{16,48},{48,16},{64,96},{96,64},{80,112},{112,80},{1... | collective-permute-start | bytes 4718600 | tf_op jit(solution)/shard_map/ppermute | solution.py:18
  187.5 6.7 copy-start.24
  192.2 1.9 copy-start.4
  207.1 13.2 %copy-start.7 = (f32[1024,256]{1,0:T(8,128)S(1)}, f32[1024,256]{1,0:T(8,128)}, u32[]{:S(2)}) copy-start(f32[1024,256]{1,0:T(8,128)} %copy.131) | copy-start | bytes 3145732
  207.1 17.7 %slice-start = ((s8[8388608]{0:T(1024)(128)(4,1)}), s8[4194304]{0:T(1024)(128)(4,1)S(1)}, s32[]{:S(2)}) async-start(s8[8388608]{0:T(1024)(128)(4,1)} %bitcast.169), calls=%async_computation.3 | async-start | bytes 8388608
  220.3 4.6 copy-start.15
  220.3 4.6 slice-start.1
  220.3 4.6 copy-start.12
  222.4 1.0 copy-start.6
  224.9 43.5 %collective-permute-start.5 = (f32[896,512]{1,0:T(8,128)}, f32[896,512]{1,0:T(8,128)}, u32[]{:S(2)}, u32[]{:S(2)}) collective-permute-start(f32[896,512]{1,0:T(8,128)} %pad_maximum_fusion), channel_id=1, source_target_pairs={{0,16},{16,0},{32,48},{48,32},{64,80},{80,64},{96,112},{112,96},{1... | collective-permute-start | bytes 5505032 | tf_op jit(solution)/shard_map/ppermute | solution.py:18
  231.6 13.3 %copy-start.37 = (bf16[512,4,64]{0,2,1:T(8,128)(2,1)S(1)}, bf16[512,4,64]{0,2,1:T(8,128)(2,1)}, u32[]{:S(2)}) copy-start(bf16[512,4,64]{0,2,1:T(8,128)(2,1)} %get-tuple-element.77) | copy-start | bytes 786436
  242.8 12.0 %copy-start.42 = (bf16[256,4,64]{0,2,1:T(8,128)(2,1)S(1)}, bf16[256,4,64]{0,2,1:T(8,128)(2,1)}, u32[]{:S(2)}) copy-start(bf16[256,4,64]{0,2,1:T(8,128)(2,1)} %get-tuple-element.73) | copy-start | bytes 393220
  266.7 4.5 copy-start.9
  266.7 6.1 copy-start.52
  268.3 2.8 copy-start.10
  268.4 4.4 copy-start.38
  271.2 3.7 copy-start.43
  271.2 3.7 copy-start.50
  272.7 3.4 copy-start.44
  272.7 3.4 copy-start.45
  272.7 3.4 copy-start.48
  274.0 4.2 copy-start.32
  275.3 6.5 copy-start.29
  275.3 6.5 copy-start.30
  310.9 708.0 %all-gather.2.cloned.1.call-start = ((), (), s32[]{:S(2)}) async-start(), calls=%async_computation.1 | async-start | bytes 1671168 | tf_op jit(solution)/shard_map/all_gather | solution.py:200
Sparse Core Ops, SparseCore 0:
  311.0 657.6 reduce-scatter.3
  971.5 47.3 all-gather.1
where the time goes:
time: 1040 us; the launch traced here: 1030 us
  waiting for transfers between devices  717 us (69%)
  matrix products  124 us (12%)
  local copies, waits for them, and re-layouts  108 us (10%)
  other arithmetic  53.5 us (5%)
  between operations  15.3 us (1%)
  starting transfers between devices  10.7 us (1%)
    reduce_scatter x1, waiting for transfers between devices, per_device(): lax.psum_scatter(lax.dot_general(inputs, d_qkv, (((0,), (0,)), ((), ())),...  658 us
    dot_general x24, matrix products, product(): return jnp.einsum(form, left, right, preferred_element_type=jnp.float32)  90.1 us
    all_gather x1, waiting for transfers between devices, per_device(): d_weights = lax.all_gather(partial_rows, 'dp', axis=0, tiled=True)  35.7 us
    unnamed x122, local copies, waits for them, and re-layouts  29.8 us
    ppermute x6, waiting for transfers between devices, partner_2(): return lax.ppermute(block, axis, route)  23.8 us
  transfers between devices with their start and end apart: 8, of which 6 were waited for; matrix products, arithmetic and copies ran while one was open for 16% of the time, Pallas kernels for 0%

commit v1 on v0

v1 whole, which is shorter than its diff:
```python
import jax
import jax.numpy as jnp
from jax import lax
from jax.experimental import pallas as pl
from jax.experimental.pallas import tpu as pltpu
from jax.sharding import PartitionSpec as P

BLK = 128
ROWS = 1024
BF = jnp.bfloat16
F32 = jnp.float32
SPANS = (1, 2, 4, 8)
CHUNK = 256
VMEM_LIMIT = 48 * 1024 * 1024


def swap(block, axis, mask):
    count = lax.axis_size(axis)
    return lax.ppermute(block, axis, [(i, i ^ mask) for i in range(count)])


def dot(left, right):
    return jnp.dot(left, right, preferred_element_type=F32)


def params(semantics=None):
    return pltpu.CompilerParams(vmem_limit_bytes=VMEM_LIMIT, dimension_semantics=semantics)


def cost(flops, nbytes):
    return pl.CostEstimate(flops=int(flops), bytes_accessed=int(nbytes), transcendentals=0)


def first_head(shape):
    return lax.broadcasted_iota(jnp.int32, shape, len(shape) - 1) < 64


def project_groups(tokens, w_qkv, incoming, scal, groups):
    total = sum(ROWS // SPANS[g] for g in groups)

    def body(scal_ref, tok_ref, w_ref, in_ref, keep_ref, send_ref, tmp_ref):
        which = pl.program_id(0)
        part = pl.program_id(1)
        tmp_ref[...] = dot(tok_ref[...], w_ref[...]).astype(BF)
        low = first_head((BLK, BLK))
        mine = scal_ref[32]

        def pick(src, slot, group, base):
            span = SPANS[group]
            for dst, pair in ((keep_ref, mine), (send_ref, 1 - mine)):
                col = pl.multiple_of(pair * BLK, BLK)
                off_a = scal_ref[group * 4 + 2 * pair]
                off_b = scal_ref[group * 4 + 2 * pair + 1]
                for r in range(8 // span):
                    row_a = pl.multiple_of((r * span + off_a) * BLK, BLK)
                    row_b = pl.multiple_of((r * span + off_b) * BLK, BLK)
                    blk_a = src[pl.ds(row_a, BLK), pl.ds(col, BLK)]
                    blk_b = src[pl.ds(row_b, BLK), pl.ds(col, BLK)]
                    dst[slot, pl.ds(base + r * BLK, BLK), :] = jnp.where(low, blk_a, blk_b)

        base = 0
        for n, group in enumerate(groups):

            @pl.when(which == n)
            def _(group=group, base=base):
                pick(tmp_ref, part, group, base)

                @pl.when(part == 0)
                def _():
                    pick(in_ref, 3, group, base)

            base += ROWS // SPANS[group]

    first = groups[0]
    out = jax.ShapeDtypeStruct((4, total, BLK), BF)
    return pl.pallas_call(
        body,
        grid_spec=pltpu.PrefetchScalarGridSpec(
            num_scalar_prefetch=1,
            grid=(len(groups), 3),
            in_specs=[
                pl.BlockSpec((ROWS, 1024), lambda i, j, s: (0, 0)),
                pl.BlockSpec((1024, 256), lambda i, j, s: (0, j * 4 + first + i)),
                pl.BlockSpec((ROWS, 256), lambda i, j, s: (0, first + i)),
            ],
            out_specs=[pl.BlockSpec((4, total, BLK), lambda i, j, s: (0, 0, 0))] * 2,
            scratch_shapes=[pltpu.VMEM((ROWS, 256), BF)],
        ),
        out_shape=[out, out],
        compiler_params=params(),
        cost_estimate=cost(len(groups) * 2 * 1024 * 1024 * 768, 6e6),
        name="project_kept",
    )(scal, tokens, w_qkv, incoming)


def project_dense(tokens, w_qkv):
    def body(tok_ref, w_ref, out_ref):
        res = dot(tok_ref[...], w_ref[...]).astype(BF)
        out_ref[0, 0] = res[:, :BLK]
        out_ref[0, 1] = res[:, BLK:]

    return pl.pallas_call(
        body,
        grid=(3,),
        in_specs=[
            pl.BlockSpec((ROWS, 1024), lambda j: (0, 0)),
            pl.BlockSpec((1024, 256), lambda j: (0, j * 4)),
        ],
        out_specs=pl.BlockSpec((1, 2, ROWS, BLK), lambda j: (j, 0, 0, 0)),
        out_shape=jax.ShapeDtypeStruct((3, 2, ROWS, BLK), BF),
        compiler_params=params(),
        cost_estimate=cost(2 * 1024 * 1024 * 768, 5e6),
        name="project_dense",
    )(tokens, w_qkv)


def pair_core(q_s, do_s, k_s, v_s, kt_s, vt_s, o_s, dq_s, dk_s, dv_s, q_rows):
    kt_s[...] = k_s[...].T
    vt_s[...] = v_s[...].T
    low_lane = first_head((CHUNK, BLK))
    low_row = lax.broadcasted_iota(jnp.int32, (BLK, CHUNK), 0) < 64
    zero = jnp.zeros((), BF)

    def step(c, _):
        rows = pl.ds(pl.multiple_of(c * CHUNK, CHUNK), CHUNK)
        q_c = q_s[rows, :] * jnp.asarray(0.125, BF)
        do_c = do_s[rows, :]
        q_t = q_c.T
        do_t = do_c.T
        outs, dqs = [], []
        d_v, d_k = None, None
        for a in range(2):
            mask = low_row if a == 0 else jnp.logical_not(low_row)
            lanes = low_lane if a == 0 else jnp.logical_not(low_lane)
            part = slice(a * 64, a * 64 + 64)
            scores = dot(k_s[...], jnp.where(mask, q_t, zero))
            top = jnp.max(scores, axis=0, keepdims=True)
            e = jnp.exp(scores - top)
            total = jnp.sum(e, axis=0, keepdims=True)
            prob = e * (1.0 / total)
            prob_b = prob.astype(BF)
            out_b = dot(vt_s[part, :], prob_b).astype(BF)
            delta = jnp.sum(
                do_t[part, :].astype(F32) * out_b.astype(F32), axis=0, keepdims=True
            )
            d_prob = dot(v_s[...], jnp.where(mask, do_t, zero))
            d_score = (prob * (d_prob - delta)).astype(BF)
            dqs.append(dot(kt_s[part, :], d_score) * 0.125)
            outs.append(out_b)
            dv_a = dot(prob_b, jnp.where(lanes, do_c, zero))
            dk_a = dot(d_score, jnp.where(lanes, q_c, zero))
            d_v = dv_a if d_v is None else d_v + dv_a
            d_k = dk_a if d_k is None else d_k + dk_a
        o_s[rows, :] = jnp.concatenate(outs, axis=0).T
        dq_s[rows, :] = jnp.concatenate(dqs, axis=0).T.astype(BF)

        @pl.when(c == 0)
        def _():
            dv_s[...] = d_v
            dk_s[...] = d_k

        @pl.when(c > 0)
        def _():
            dv_s[...] += d_v
            dk_s[...] += d_k

        return 0

    lax.fori_loop(0, q_rows // CHUNK, step, 0)


def attention_scratch(q_rows):
    return [
        pltpu.VMEM((q_rows, BLK), BF),
        pltpu.VMEM((q_rows, BLK), BF),
        pltpu.VMEM((ROWS, BLK), BF),
        pltpu.VMEM((ROWS, BLK), BF),
        pltpu.VMEM((BLK, ROWS), BF),
        pltpu.VMEM((BLK, ROWS), BF),
        pltpu.VMEM((q_rows, BLK), BF),
        pltpu.VMEM((q_rows, BLK), BF),
        pltpu.VMEM((ROWS, BLK), F32),
        pltpu.VMEM((ROWS, BLK), F32),
    ]


HEAD_FLOPS = 6 * 2 * 1024 * 1024 * 256


def attention_dense(qkv, incoming, pair):
    def body(qkv_ref, do_ref, out_ref, kt_s, vt_s, dk_s, dv_s):
        pair_core(
            qkv_ref.at[0, 0], do_ref, qkv_ref.at[1, 0], qkv_ref.at[2, 0], kt_s, vt_s,
            out_ref.at[0], out_ref.at[1], dk_s, dv_s, ROWS,
        )
        out_ref[2] = dk_s[...].astype(BF)
        out_ref[3] = dv_s[...].astype(BF)

    return pl.pallas_call(
        body,
        grid=(1,),
        in_specs=[
            pl.BlockSpec((3, 1, ROWS, BLK), lambda i: (0, pair, 0, 0)),
            pl.BlockSpec((ROWS, BLK), lambda i: (0, pair)),
        ],
        out_specs=pl.BlockSpec((4, ROWS, BLK), lambda i: (0, 0, 0)),
        out_shape=jax.ShapeDtypeStruct((4, ROWS, BLK), BF),
        scratch_shapes=attention_scratch(ROWS)[4:6] + attention_scratch(ROWS)[8:],
        compiler_params=params(),
        cost_estimate=cost(2 * HEAD_FLOPS, 2e6),
        name="attention_dense",
    )(qkv, incoming)


def attention_two(keep, recv):
    half = ROWS // 2

    def body(keep_ref, recv_ref, own_ref, back_ref, *scratch):
        q_s, do_s, k_s, v_s, kt_s, vt_s, o_s, dq_s, dk_s, dv_s = scratch
        for slot, dst in ((0, q_s), (1, k_s), (2, v_s), (3, do_s)):
            dst[:half, :] = keep_ref[slot]
            dst[half:, :] = recv_ref[slot]
        pair_core(q_s, do_s, k_s, v_s, kt_s, vt_s, o_s, dq_s, dk_s, dv_s, ROWS)
        for slot, src in ((0, o_s), (1, dq_s), (2, dk_s), (3, dv_s)):
            own_ref[slot] = src[:half, :].astype(BF)
            back_ref[slot] = src[half:, :].astype(BF)

    out = jax.ShapeDtypeStruct((4, half, BLK), BF)
    return pl.pallas_call(
        body,
        out_shape=[out, out],
        scratch_shapes=attention_scratch(ROWS),
        compiler_params=params(),
        cost_estimate=cost(2 * HEAD_FLOPS, 2e6),
        name="attention_two",
    )(keep, recv)


def attention_wide(keep, recv, from_2, from_4, from_6):
    def body(
        keep_ref, recv_ref, f2_ref, f4_ref, f6_ref,
        oq2_ref, loc2_ref, oq3_ref, loc3_ref, to2_ref, to4_ref, to6_ref, *scratch,
    ):
        q_s, do_s, k_s, v_s, kt_s, vt_s, o_s, dq_s, dk_s, dv_s = scratch
        for slot, dst in ((0, q_s), (3, do_s)):
            dst[0:256, :] = keep_ref[slot, 0:256, :]
            dst[256:512, :] = recv_ref[slot, 0:256, :]
        for n, dst in ((0, k_s), (1, v_s)):
            dst[0:256, :] = keep_ref[1 + n, 0:256, :]
            dst[256:512, :] = recv_ref[1 + n, 0:256, :]
            dst[512:, :] = f2_ref[n, 0:512, :]
        pair_core(q_s, do_s, k_s, v_s, kt_s, vt_s, o_s, dq_s, dk_s, dv_s, 512)
        oq2_ref[0] = o_s[...]
        oq2_ref[1] = dq_s[...]
        for n, src in ((0, dk_s), (1, dv_s)):
            loc2_ref[n] = src[:512, :]
            to2_ref[n, 0:512, :] = src[512:, :].astype(BF)
        for slot, dst in ((0, q_s), (3, do_s)):
            dst[0:128, :] = keep_ref[slot, 256:384, :]
            dst[128:256, :] = recv_ref[slot, 256:384, :]
        for n, dst in ((0, k_s), (1, v_s)):
            dst[0:128, :] = keep_ref[1 + n, 256:384, :]
            dst[128:256, :] = recv_ref[1 + n, 256:384, :]
            dst[256:512, :] = f2_ref[n, 512:768, :]
            dst[512:768, :] = f4_ref[n]
            dst[768:, :] = f6_ref[n]
        pair_core(q_s, do_s, k_s, v_s, kt_s, vt_s, o_s, dq_s, dk_s, dv_s, 256)
        oq3_ref[0] = o_s[:256, :]
        oq3_ref[1] = dq_s[:256, :]
        for n, src in ((0, dk_s), (1, dv_s)):
            loc3_ref[n] = src[:256, :]
            to2_ref[n, 512:768, :] = src[256:512, :].astype(BF)
            to4_ref[n] = src[512:768, :].astype(BF)
            to6_ref[n] = src[768:, :].astype(BF)

    shapes = [
        ((2, 512, BLK), BF), ((2, 512, BLK), F32), ((2, 256, BLK), BF), ((2, 256, BLK), F32),
        ((2, 768, BLK), BF), ((2, 256, BLK), BF), ((2, 256, BLK), BF),
    ]
    return pl.pallas_call(
        body,
        out_shape=[jax.ShapeDtypeStruct(s, d) for s, d in shapes],
        scratch_shapes=attention_scratch(512),
        compiler_params=params(),
        cost_estimate=cost(1.5 * HEAD_FLOPS, 2e6),
        name="attention_wide",
    )(keep, recv, from_2, from_4, from_6)


def combine_wide(oq2, loc2, oq3, loc3, ret2, ret4, ret6):
    def body(oq2_ref, loc2_ref, oq3_ref, loc3_ref, r2_ref, r4_ref, r6_ref, own_ref, back_ref):
        for dst, at2, at3 in ((own_ref, 0, 0), (back_ref, 256, 128)):
            two = slice(at2, at2 + 256)
            three = slice(at3, at3 + 128)
            for n in range(2):
                dst[n, 0:256, :] = oq2_ref[n, two, :]
                dst[n, 256:384, :] = oq3_ref[n, three, :]
                dst[2 + n, 0:256, :] = (loc2_ref[n, two, :] + r2_ref[n, two, :].astype(F32)).astype(BF)
                far = r4_ref[n, three, :].astype(F32) + r6_ref[n, three, :].astype(F32)
                near = r2_ref[n, 512 + at3 : 640 + at3, :].astype(F32)
                dst[2 + n, 256:384, :] = (loc3_ref[n, three, :] + near + far).astype(BF)

    out = jax.ShapeDtypeStruct((4, 384, BLK), BF)
    return pl.pallas_call(
        body,
        out_shape=[out, out],
        compiler_params=params(),
        cost_estimate=cost(1e6, 2e6),
        name="combine_wide",
    )(oq2, loc2, oq3, loc3, ret2, ret4, ret6)


def block_mask(block, span, off_a, off_b, low):
    here = block % span
    keep_a = jnp.where(off_a == here, 1, 0)
    keep_b = jnp.where(off_b == here, 1, 0)
    return jnp.where(low, keep_a, keep_b) == 1


def weight_grad(tokens, tokens_other, mine, other, scal, group, base, table):
    span = SPANS[group]

    def body(scal_ref, tok_ref, tok2_ref, mine_ref, other_ref, send_ref, keep_ref, g_s):
        i = pl.program_id(0)

        @pl.when(i == 0)
        def _():
            low = first_head((BLK, BLK))
            pair = scal_ref[33]
            for n, src in ((0, mine_ref), (1, other_ref)):
                off_a = scal_ref[n * 16 + group * 4 + 2 * pair]
                off_b = scal_ref[n * 16 + group * 4 + 2 * pair + 1]
                for block in range(8):
                    mask = block_mask(block, span, off_a, off_b, low)
                    row = base + (block // span) * BLK
                    for part in range(3):
                        val = src[part, row : row + BLK, :]
                        g_s[n * ROWS + block * BLK : n * ROWS + block * BLK + BLK,
                            part * BLK : part * BLK + BLK] = jnp.where(mask, val, jnp.zeros((), BF))

        over_rows = (((0,), (0,)), ((), ()))
        res = lax.dot_general(tok_ref[...], g_s[:ROWS, :], over_rows, preferred_element_type=F32)
        res += lax.dot_general(tok2_ref[...], g_s[ROWS:, :], over_rows, preferred_element_type=F32)

        @pl.when(i < 2)
        def _():
            send_ref[0] = res.astype(BF)

        @pl.when(i >= 2)
        def _():
            keep_ref[0] = res

    slab = mine.shape[1]
    return pl.pallas_call(
        body,
        grid_spec=pltpu.PrefetchScalarGridSpec(
            num_scalar_prefetch=1,
            grid=(4,),
            in_specs=[
                pl.BlockSpec((ROWS, 256), lambda i, s: (0, s[table + i])),
                pl.BlockSpec((ROWS, 256), lambda i, s: (0, s[table + i])),
                pl.BlockSpec((3, slab, BLK), lambda i, s: (0, 0, 0)),
                pl.BlockSpec((3, slab, BLK), lambda i, s: (0, 0, 0)),
            ],
            out_specs=[
                pl.BlockSpec((1, 256, 384), lambda i, s: (jnp.minimum(i, 1), 0, 0)),
                pl.BlockSpec((1, 256, 384), lambda i, s: (jnp.maximum(i - 2, 0), 0, 0)),
            ],
            scratch_shapes=[pltpu.VMEM((2 * ROWS, 384), BF)],
        ),
        out_shape=[
            jax.ShapeDtypeStruct((2, 256, 384), BF),
            jax.ShapeDtypeStruct((2, 256, 384), F32),
        ],
        compiler_params=params(),
        cost_estimate=cost(2 * 1024 * 2048 * 384, 5e6),
        name="weight_grad",
    )(scal, tokens, tokens_other, mine, other)


def token_grad(w_qkv, scal, dense, one, wide):
    def body(scal_ref, w_ref, d0_ref, d1_ref, o1_ref, r1_ref, ow_ref, rw_ref, att_ref, dx_ref, g_s):
        i = pl.program_id(0)

        @pl.when(i == 0)
        def _():
            low = first_head((BLK, BLK))
            zero = jnp.zeros((), BF)
            mine = scal_ref[32]
            for part in range(4):
                for pair, src in ((0, d0_ref), (1, d1_ref)):
                    if part == 0:
                        att_ref[:, pair * BLK : pair * BLK + BLK] = src[0]
                    else:
                        col = (part - 1) * 1024 + pair * BLK
                        g_s[:, col : col + BLK] = src[part]
            for group, base, own, ret in ((1, 0, o1_ref, r1_ref), (2, 0, ow_ref, rw_ref), (3, 256, ow_ref, rw_ref)):
                span = SPANS[group]
                for src, pair in ((own, mine), (ret, 1 - mine)):
                    off_a = scal_ref[group * 4 + 2 * pair]
                    off_b = scal_ref[group * 4 + 2 * pair + 1]
                    for block in range(8):
                        mask = block_mask(block, span, off_a, off_b, low)
                        row = base + (block // span) * BLK
                        rows = slice(block * BLK, block * BLK + BLK)
                        for part in range(4):
                            val = jnp.where(mask, src[part, row : row + BLK, :], zero)
                            col = group * 256 + pair * BLK
                            if part == 0:
                                att_ref[rows, pl.ds(pl.multiple_of(col, BLK), BLK)] = val
                            else:
                                col = col + (part - 1) * 1024
                                g_s[rows, pl.ds(pl.multiple_of(col, BLK), BLK)] = val

        dx_ref[...] = lax.dot_general(
            g_s[...], w_ref[...], (((1,), (1,)), ((), ())), preferred_element_type=F32
        ).astype(BF)

    def whole(shape):
        return pl.BlockSpec(shape, lambda i, s: (0,) * len(shape))

    out = jax.ShapeDtypeStruct((ROWS, 1024), BF)
    return pl.pallas_call(
        body,
        grid_spec=pltpu.PrefetchScalarGridSpec(
            num_scalar_prefetch=1,
            grid=(4,),
            in_specs=[
                pl.BlockSpec((256, 3072), lambda i, s: (i, 0)),
                whole((4, ROWS, BLK)), whole((4, ROWS, BLK)),
                whole((4, 512, BLK)), whole((4, 512, BLK)),
                whole((4, 384, BLK)), whole((4, 384, BLK)),
            ],
            out_specs=[
                pl.BlockSpec((ROWS, 1024), lambda i, s: (0, 0)),
                pl.BlockSpec((ROWS, 256), lambda i, s: (0, i)),
            ],
            scratch_shapes=[pltpu.VMEM((ROWS, 3072), BF)],
        ),
        out_shape=[out, out],
        compiler_params=params(),
        cost_estimate=cost(2 * 1024 * 1024 * 3072, 12e6),
        name="token_grad",
    )(scal, w_qkv, dense[0], dense[1], one[0], one[1], wide[0], wide[1])


def per_device(tokens, w_qkv, offsets, d_attended):
    inputs = tokens[0]
    incoming = d_attended[0]
    seq = lax.axis_index("seq")
    core = lax.axis_index("dp") & 1
    b0, b1, b2 = seq & 1, (seq >> 1) & 1, (seq >> 2) & 1
    gray = b1 ^ b2

    def start_p(j, f):
        return 2 * j + (f ^ j)

    def start_q(j, f):
        return 2 * f + j

    tail = [b0, core]
    tail += [start_p(0, 1 - gray), start_p(1, 1 - gray), start_p(0, gray), start_p(1, gray)]
    tail += [start_q(0, 1 - b2), start_q(1, 1 - b2), start_q(0, b2), start_q(1, b2)]
    tail = [jnp.asarray(t, jnp.int32) for t in tail]
    row = offsets[0]
    row_other = swap(row, "dp", 1)
    scal_own = jnp.concatenate([row, row, jnp.stack(tail)])
    scal = jnp.concatenate([row, row_other, jnp.stack(tail)])
    table_p, table_q = 34, 38

    inputs_other = swap(inputs, "dp", 1)

    keep_w, send_w = project_groups(inputs, w_qkv, incoming, scal_own, (2, 3))
    recv_w = swap(send_w, "seq", 1)
    keep_1, send_1 = project_groups(inputs, w_qkv, incoming, scal_own, (1,))
    recv_1 = swap(send_1, "seq", 1)
    qkv_0 = project_dense(inputs, w_qkv)

    kv_3 = jnp.concatenate([keep_w[1:3, 256:], recv_w[1:3, 256:]], axis=1)
    kv_2 = jnp.concatenate([keep_w[1:3, :256], recv_w[1:3, :256], kv_3], axis=1)
    from_2 = swap(kv_2, "seq", 2)
    from_4 = swap(kv_3, "seq", 4)
    from_6 = swap(kv_3, "seq", 6)

    dense = [attention_dense(qkv_0, incoming, pair) for pair in range(2)]

    oq2, loc2, oq3, loc3, to2, to4, to6 = attention_wide(keep_w, recv_w, from_2, from_4, from_6)
    ret2 = swap(to2, "seq", 2)
    ret4 = swap(to4, "seq", 4)
    ret6 = swap(to6, "seq", 6)
    own_1, back_1 = attention_two(keep_1, recv_1)
    ret_1 = swap(back_1, "seq", 1)
    own_w, back_w = combine_wide(oq2, loc2, oq3, loc3, ret2, ret4, ret6)
    ret_w = swap(back_w, "seq", 1)

    def halves(first, second, same):
        mine = jnp.where(same, first[1:], second[1:])
        other = jnp.where(same, second[1:], first[1:])
        return mine, swap(other, "dp", 1)

    def reduce_seq(send, keep, kind):
        near, far, bit = (2, 6, b2) if kind == 0 else (6, 2, b1)
        total = keep + swap(send, "seq", near).astype(F32)
        leave = jnp.where(bit == 0, total[1], total[0]).astype(BF)
        stay = jnp.where(bit == 0, total[0], total[1])
        return stay + swap(leave, "seq", far).astype(F32)

    def finish(parts):
        total = jnp.concatenate(parts, axis=1)
        leave = jnp.where(b0 == 0, total[128:], total[:128]).astype(BF)
        stay = jnp.where(b0 == 0, total[:128], total[128:])
        total = stay + swap(leave, "seq", 1).astype(F32)
        for mask in (2, 6, 8):
            half = total.astype(BF)
            total = half.astype(F32) + swap(half, "dp", mask).astype(F32)
        return total

    mine_0, other_0 = halves(dense[0], dense[1], core == 0)
    send, keep = weight_grad(inputs, inputs_other, mine_0, other_0, scal, 0, 0, table_p)
    part_0 = reduce_seq(send, keep, 0)
    mine_1, other_1 = halves(own_1, ret_1, core == b0)
    send, keep = weight_grad(inputs, inputs_other, mine_1, other_1, scal, 1, 0, table_q)
    part_1 = reduce_seq(send, keep, 1)
    done_01 = finish([part_0, part_1])
    mine_w, other_w = halves(own_w, ret_w, core == b0)
    send, keep = weight_grad(inputs, inputs_other, mine_w, other_w, scal, 2, 0, table_p)
    part_2 = reduce_seq(send, keep, 0)
    send, keep = weight_grad(inputs, inputs_other, mine_w, other_w, scal, 3, 256, table_q)
    part_3 = reduce_seq(send, keep, 1)
    done_23 = finish([part_2, part_3])

    attended, d_inputs = token_grad(w_qkv, scal_own, dense, (own_1, ret_1), (own_w, ret_w))

    done = jnp.concatenate([done_01, done_23], axis=1)
    done_other = swap(done, "dp", 1)
    low = jnp.where(core == 0, done, done_other).reshape(128, 4, 3, 128)
    high = jnp.where(core == 0, done_other, done).reshape(128, 4, 3, 128)
    both = jnp.stack([low, high], axis=3)
    d_weights = jnp.transpose(both, (0, 2, 1, 3, 4)).reshape(128, 3072)
    return (attended[None], d_inputs[None], d_weights)


def solution(mesh):
    placed = (P("dp", "seq", None), P(), P("dp", None), P("dp", "seq", None))
    return jax.shard_map(
        per_device,
        mesh=mesh,
        in_specs=placed,
        out_specs=(P("dp", "seq", None), P("dp", "seq", None), P("seq", None)),
        check_vma=False,
    )
```

time: 1040 us -> 213 us (0.20); the launches traced: 1030 us -> 213 us
  waiting for transfers between devices: 717 us -> 41.3 us
  matrix products: 124 us -> 0 us
  Pallas kernels: 0 us -> 103 us
  local copies, waits for them, and re-layouts: 108 us -> 11.6 us
  other arithmetic: 53.5 us -> 5.59 us
  starting transfers between devices: 10.7 us -> 50.3 us
  between operations: 15.3 us -> 1.07 us
    reduce_scatter x1 -> x0, waiting for transfers between devices: 658 us -> none  [per_device(): lax.psum_scatter(lax.dot_general(inputs, d_qkv, (((0,), (0,)), ((), ())),...]
    dot_general x27 -> x0, matrix products: 124 us -> none  [the longest x24 90.1 us: product(): return jnp.einsum(form, left, right, preferred_element_type=jnp.float32)]
    pallas_call x0 -> x13, Pallas kernels: none -> 103 us  [the longest x2 26.5 us: attention_dense(): pl.pallas_call(body, grid=(1,), in_specs=[pl.BlockSpec((3, 1, ROWS, BLK),...]
    ppermute x6 -> x32, starting transfers between devices: 10.6 us -> 50.3 us  [swap(): return lax.ppermute(block, axis, [(i, i ^ mask) for i in range(count)])]
    all_gather x1 -> x0, waiting for transfers between devices: 35.7 us -> none  [per_device(): d_weights = lax.all_gather(partial_rows, 'dp', axis=0, tiled=True)]
    slice x24 -> x4, local copies, waits for them, and re-layouts: 24 us -> 0.74 us  [the longest x2 0.73 us: per_device(): kv_2 = jnp.concatenate([keep_w[1:3, :256], recv_w[1:3, :256], kv_3], axis=1)]
    unnamed x122 -> x31, local copies, waits for them, and re-layouts: 29.8 us -> 9.27 us
    ppermute x6 -> x32, waiting for transfers between devices: 23.8 us -> 41.3 us  [swap(): return lax.ppermute(block, axis, [(i, i ^ mask) for i in range(count)])]
  transfers between devices with their start and end apart: 8 -> 32, of which waited for: 6 -> 13; matrix products, arithmetic and copies ran while one was open for 16% -> 3% of each run, Pallas kernels for 0% -> 48%
where the time goes in v1:
time: 213 us
  Pallas kernels  103 us (48%)
  starting transfers between devices  50.3 us (24%)
  waiting for transfers between devices  41.3 us (19%)
  local copies, waits for them, and re-layouts  11.6 us (5%)
  other arithmetic  5.59 us (3%)
    ppermute x32, starting transfers between devices, swap(): return lax.ppermute(block, axis, [(i, i ^ mask) for i in range(count)])  50.3 us
    ppermute x32, waiting for transfers between devices, swap(): return lax.ppermute(block, axis, [(i, i ^ mask) for i in range(count)])  41.3 us
    pallas_call x2, Pallas kernels, attention_dense(): pl.pallas_call(body, grid=(1,), in_specs=[pl.BlockSpec((3, 1, ROWS, BLK),...  26.5 us
    pallas_call x4, Pallas kernels, weight_grad(): pl.pallas_call(body, grid_spec=pltpu.PrefetchScalarGridSpec(num_scalar_pr...  22.4 us
    pallas_call x1, Pallas kernels, attention_two(): pl.pallas_call(body, out_shape=[out, out], scratch_shapes=attention_scrat...  14 us
    pallas_call x2, Pallas kernels, project_groups(): pl.pallas_call(body, grid_spec=pltpu.PrefetchScalarGridSpec(num_scalar_pr...  12.8 us
    pallas_call x1, Pallas kernels, token_grad(): pl.pallas_call(body, grid_spec=pltpu.PrefetchScalarGridSpec(num_scalar_pr...  12.7 us
    pallas_call x1, Pallas kernels, attention_wide(): pl.pallas_call(body, out_shape=[jax.ShapeDtypeStruct(s, d) for s, d in sh...  9.79 us
  transfers between devices with their start and end apart: 32, of which 13 were waited for; matrix products, arithmetic and copies ran while one was open for 3% of the time, Pallas kernels for 48%

profile of v1, /device:TPU:1, one launch (start us, length us, event | category | flops | bytes accessed | tf_op | source)
XLA Modules:
  0.0 212.6 jit_solution(9994471120598790730)
XLA Ops:
  0.6 1.5 collective-permute-start.11
  2.1 0.8 concatenate.22.scal_ref
  3.0 1.6 copy-done
  4.5 1.6 copy-done.2
  6.1 5.1 %project_kept.2 = (bf16[4,512,128]{2,1,0:T(8,128)(2,1)S(1)}, bf16[4,512,128]{2,1,0:T(8,128)(2,1)}) custom-call(s32[42]{0:T(128)S(1)} %concatenate.22.scal_ref, bf16[1024,1024]{1,0:T(8,128)(2,1)S(1)} %bitcast.37, bf16[1024,3072]{1,0:T(8,128)(2,1)} %w_ref.7, bf16[1024,1024]{1,0:T(8,128)(2,1)S(1)} %bitcast.44), custom_call_target="tpu_custom_call" | custom-call | flops 1610612736 | bytes 6000000 | tf_op jit(solution)/shard_map/project_kept/pallas_call | solution.py:76
  11.3 0.8 copy-done.10
  12.1 1.4 collective-permute-start
  13.4 7.6 %project_kept.3 = (bf16[4,384,128]{2,1,0:T(8,128)(2,1)S(1)}, bf16[4,384,128]{2,1,0:T(8,128)(2,1)}) custom-call(s32[42]{0:T(128)S(1)} %concatenate.22.scal_ref, bf16[1024,1024]{1,0:T(8,128)(2,1)S(1)} %bitcast.38, bf16[1024,3072]{1,0:T(8,128)(2,1)} %w_ref.7, bf16[1024,1024]{1,0:T(8,128)(2,1)S(1)} %bitcast.45), custom_call_target="tpu_custom_call" | custom-call | flops 3221225472 | bytes 6000000 | tf_op jit(solution)/shard_map/project_kept/pallas_call | solution.py:76
  21.2 3.7 %project_dense.1.qkv_ref = bf16[3,2,1024,128]{3,2,1,0:T(8,128)(2,1)S(1)} custom-call(bf16[1024,1024]{1,0:T(8,128)(2,1)S(1)} %bitcast.39, bf16[1024,3072]{1,0:T(8,128)(2,1)} %w_ref.7), custom_call_target="tpu_custom_call" | custom-call | flops 1610612736 | bytes 5000000 | tf_op jit(solution)/shard_map/project_dense/pallas_call | solution.py:102
  24.9 13.2 %attention_dense.2.d0_ref = bf16[4,1024,128]{2,1,0:T(8,128)(2,1)S(1)} custom-call(bf16[3,2,1024,128]{3,2,1,0:T(8,128)(2,1)S(1)} %project_dense.1.qkv_ref, bf16[1024,1024]{1,0:T(8,128)(2,1)S(1)} %bitcast.46), custom_call_target="tpu_custom_call" | custom-call | flops 6442450944 | bytes 2000000 | tf_op jit(solution)/shard_map/attention_dense/pallas_call | solution.py:199
  38.1 13.2 %attention_dense.3.d1_ref = bf16[4,1024,128]{2,1,0:T(8,128)(2,1)S(1)} custom-call(bf16[3,2,1024,128]{3,2,1,0:T(8,128)(2,1)S(1)} %project_dense.1.qkv_ref, bf16[1024,1024]{1,0:T(8,128)(2,1)S(1)} %bitcast.47), custom_call_target="tpu_custom_call" | custom-call | flops 6442450944 | bytes 2000000 | tf_op jit(solution)/shard_map/attention_dense/pallas_call | solution.py:199
  51.4 0.7 slice.84
  52.1 2.9 %collective-permute-start.4 = (bf16[2,256,128]{2,1,0:T(8,128)(2,1)S(1)}, bf16[2,256,128]{2,1,0:T(8,128)(2,1)S(1)}, u32[]{:S(2)}, u32[]{:S(2)}) collective-permute-start(bf16[2,256,128]{2,1,0:T(8,128)(2,1)S(1)} %pad_maximum_fusion.4), channel_id=1, source_target_pairs={{0,64},{16,80},{32,96},{48,112},{64,0},{80,16},{96,32},{112,48},{1... | collective-permute-start | bytes 393224 | tf_op jit(solution)/shard_map/ppermute | solution.py:19
  55.0 0.9 collective-permute-start.5
  55.9 0.9 pad_maximum_fusion.3
  57.1 0.8 copy-done.12
  57.9 1.0 copy-done.11
  59.0 1.0 copy-done.13
  60.0 14.0 %attention_two.1 = (bf16[4,512,128]{2,1,0:T(8,128)(2,1)S(1)}, bf16[4,512,128]{2,1,0:T(8,128)(2,1)}) custom-call(bf16[4,512,128]{2,1,0:T(8,128)(2,1)S(1)} %copy-done.11, bf16[4,512,128]{2,1,0:T(8,128)(2,1)S(1)} %copy-done.13), custom_call_target="tpu_custom_call" | custom-call | flops 6442450944 | bytes 2000000 | tf_op jit(solution)/shard_map/attention_two/pallas_call | solution.py:229
  74.0 1.2 collective-permute-start.1
  75.2 9.8 %attention_wide.1 = (bf16[2,512,128]{2,1,0:T(8,128)(2,1)S(1)}, f32[2,512,128]{2,1,0:T(8,128)S(1)}, bf16[2,256,128]{2,1,0:T(8,128)(2,1)S(1)}, f32[2,256,128]{2,1,...) custom-call(bf16[4,384,128]{2,1,0:T(8,128)(2,1)S(1)} %get-tuple-elem, ...), custom_call_target="tpu_custom_call" | custom-call | flops 4831838208 | bytes 2000000 | tf_op jit(solution)/shard_map/attention_wide/pallas_call | solution.py:280
  85.0 1.5 collective-permute-start.6
  86.5 1.6 collective-permute-start.7
  88.1 1.0 broadcast_select_fusion
  89.1 2.0 collective-permute-start.12
  91.1 7.1 %collective-permute-done.7.r4_ref = bf16[2,256,128]{2,1,0:T(8,128)(2,1)S(1)} collective-permute-done((bf16[2,256,128]{2,1,0:T(8,128)(2,1)S(1)}, bf16[2,256,128]{2,1,0:T(8,128)(2,1)S(1)}, u32[]{:S(2)}, u32[]{:S(2)}) %collective-permute-start.7) | collective-permute-done | bytes 131104 | tf_op jit(solution)/shard_map/ppermute | solution.py:19
  98.3 0.9 collective-permute-start.8
  99.1 4.2 %collective-permute-done.8.r6_ref = bf16[2,256,128]{2,1,0:T(8,128)(2,1)S(1)} collective-permute-done((bf16[2,256,128]{2,1,0:T(8,128)(2,1)S(1)}, bf16[2,256,128]{2,1,0:T(8,128)(2,1)S(1)}, u32[]{:S(2)}, u32[]{:S(2)}) %collective-permute-start.8) | collective-permute-done | bytes 131104 | tf_op jit(solution)/shard_map/ppermute | solution.py:19
  103.3 0.8 combine_wide.1
  104.2 0.8 copy-done.8
  105.1 4.2 %collective-permute-start.10 = (s32[16]{0:T(128)S(1)}, s32[16]{0:T(128)S(1)}, u32[]{:S(2)}, u32[]{:S(2)}) collective-permute-start(s32[16]{0:T(128)S(1)} %bitcast.53), channel_id=1, source_target_pairs={{0,1},{1,0},{2,3},{3,2},{4,5},{5,4},{6,7},{7,6},{8,9},{9,8},{10,11... | collective-permute-start | bytes 200 | tf_op jit(solution)/shard_map/ppermute | solution.py:19
  109.3 0.8 collective-permute-done.10
  110.2 1.1 broadcast_select_fusion.2
  111.3 0.4 collective-permute-start.15
  111.9 1.1 broadcast_select_fusion.6
  113.0 5.3 %collective-permute-start.22 = (bf16[3,384,128]{2,1,0:T(8,128)(2,1)S(1)}, bf16[3,384,128]{2,1,0:T(8,128)(2,1)S(1)}, u32[]{:S(2)}, u32[]{:S(2)}) collective-permute-start(bf16[3,384,128]{2,1,0:T(8,128)(2,1)S(1)} %get-tuple-element.62), channel_id=1, source_target_pairs={{0,1},{1,0},{2,3},{3,2},{4,5},{5,4},{6,7},{7,6},{8,9},{9,8},{10,11... | collective-permute-start | bytes 884744 | tf_op jit(solution)/shard_map/ppermute | solution.py:19
  118.2 5.9 %weight_grad.4 = (bf16[2,256,384]{2,1,0:T(8,128)(2,1)S(1)}, f32[2,256,384]{2,1,0:T(8,128)S(1)}) custom-call(s32[42]{0:T(128)S(1)} %concatenate.25.scal_ref, bf16[1024,1024]{1,0:T(8,128)(2,1)S(1)} %bitcast.40, bf16[1024,1024]{1,0:T(8,128)(2,1)} %collective-permute-done.11.tok2_ref, bf16[3,1024,128]{2,1,0:T(8,128)(2,1)S(1)} %get-tuple-element.57.mine_ref, ...), custom_call_target="tpu_custom_call" | custom-call | flops 1610612736 | bytes 5000000 | tf_op jit(solution)/shard_map/weight_grad/pallas_call | solution.py:354
  124.2 5.5 %weight_grad.5 = (bf16[2,256,384]{2,1,0:T(8,128)(2,1)S(1)}, f32[2,256,384]{2,1,0:T(8,128)S(1)}) custom-call(s32[42]{0:T(128)S(1)} %concatenate.25.scal_ref, bf16[1024,1024]{1,0:T(8,128)(2,1)S(1)} %bitcast.41, bf16[1024,1024]{1,0:T(8,128)(2,1)} %collective-permute-done.11.tok2_ref, bf16[3,512,128]{2,1,0:T(8,128)(2,1)S(1)} %get-tuple-element.61.mine_ref, ...), custom_call_target="tpu_custom_call" | custom-call | flops 1610612736 | bytes 5000000 | tf_op jit(solution)/shard_map/weight_grad/pallas_call | solution.py:354
  129.8 0.9 collective-permute-start.16
  130.7 5.5 %weight_grad.6 = (bf16[2,256,384]{2,1,0:T(8,128)(2,1)S(1)}, f32[2,256,384]{2,1,0:T(8,128)S(1)}) custom-call(s32[42]{0:T(128)S(1)} %concatenate.25.scal_ref, bf16[1024,1024]{1,0:T(8,128)(2,1)S(1)} %bitcast.42, bf16[1024,1024]{1,0:T(8,128)(2,1)} %collective-permute-done.11.tok2_ref, bf16[3,384,128]{2,1,0:T(8,128)(2,1)S(1)} %get-tuple-element.63.mine_ref, ...), custom_call_target="tpu_custom_call" | custom-call | flops 1610612736 | bytes 5000000 | tf_op jit(solution)/shard_map/weight_grad/pallas_call | solution.py:354
  136.2 0.9 collective-permute-start.23
  137.1 5.5 %weight_grad.7 = (bf16[2,256,384]{2,1,0:T(8,128)(2,1)S(1)}, f32[2,256,384]{2,1,0:T(8,128)S(1)}) custom-call(s32[42]{0:T(128)S(1)} %concatenate.25.scal_ref, bf16[1024,1024]{1,0:T(8,128)(2,1)S(1)} %bitcast.43, bf16[1024,1024]{1,0:T(8,128)(2,1)} %collective-permute-done.11.tok2_ref, bf16[3,384,128]{2,1,0:T(8,128)(2,1)S(1)} %get-tuple-element.63.mine_ref, ...), custom_call_target="tpu_custom_call" | custom-call | flops 1610612736 | bytes 5000000 | tf_op jit(solution)/shard_map/weight_grad/pallas_call | solution.py:354
  142.7 1.9 collective-permute-start.25
  144.7 0.9 collective-permute-start.14
  145.8 0.9 collective-permute-done.23
  146.8 1.9 collective-permute-start.24
  148.7 5.0 %collective-permute-done.25 = bf16[2,256,384]{2,1,0:T(8,128)(2,1)S(1)} collective-permute-done((bf16[2,256,384]{2,1,0:T(8,128)(2,1)S(1)}, bf16[2,256,384]{2,1,0:T(8,128)(2,1)S(1)}, u32[]{:S(2)}, u32[]{:S(2)}) %collective-permute-start.25) | collective-permute-done | bytes 393248 | tf_op jit(solution)/shard_map/ppermute | solution.py:19
  153.9 4.0 %collective-permute-done.14 = bf16[256,384]{1,0:T(8,128)(2,1)S(1)} collective-permute-done((bf16[256,384]{1,0:T(8,128)(2,1)S(1)}, bf16[256,384]{1,0:T(8,128)(2,1)S(1)}, u32[]{:S(2)}, u32[]{:S(2)}) %collective-permute-start.14) | collective-permute-done | bytes 196640 | tf_op jit(solution)/shard_map/ppermute | solution.py:19
  158.1 0.4 collective-permute-start.18
  158.5 3.7 %collective-permute-done.24 = bf16[256,384]{1,0:T(8,128)(2,1)S(1)} collective-permute-done((bf16[256,384]{1,0:T(8,128)(2,1)S(1)}, bf16[256,384]{1,0:T(8,128)(2,1)S(1)}, u32[]{:S(2)}, u32[]{:S(2)}) %collective-permute-start.24) | collective-permute-done | bytes 196640 | tf_op jit(solution)/shard_map/ppermute | solution.py:19
  162.3 0.4 collective-permute-start.27
  163.0 1.7 collective-permute-start.19
  164.8 4.5 %collective-permute-done.27 = bf16[128,768]{1,0:T(8,128)(2,1)S(1)} collective-permute-done((bf16[128,768]{1,0:T(8,128)(2,1)S(1)}, bf16[128,768]{1,0:T(8,128)(2,1)S(1)}, u32[]{:S(2)}, u32[]{:S(2)}) %collective-permute-start.27) | collective-permute-done | bytes 196640 | tf_op jit(solution)/shard_map/ppermute | solution.py:19
  169.3 1.7 collective-permute-start.28
  171.1 2.3 %collective-permute-start.20 = (bf16[128,768]{1,0:T(8,128)(2,1)S(1)}, bf16[128,768]{1,0:T(8,128)(2,1)S(1)}, u32[]{:S(2)}, u32[]{:S(2)}) collective-permute-start(bf16[128,768]{1,0:T(8,128)(2,1)S(1)} %add_convert_fusion.4), channel_id=1, source_target_pairs={{0,6},{1,7},{2,4},{3,5},{4,2},{5,3},{6,0},{7,1},{8,14},{9,15},{10,... | collective-permute-start | bytes 589832 | tf_op jit(solution)/shard_map/ppermute | solution.py:19
  173.4 3.0 %collective-permute-done.28 = bf16[128,768]{1,0:T(8,128)(2,1)S(1)} collective-permute-done((bf16[128,768]{1,0:T(8,128)(2,1)S(1)}, bf16[128,768]{1,0:T(8,128)(2,1)S(1)}, u32[]{:S(2)}, u32[]{:S(2)}) %collective-permute-start.28) | collective-permute-done | bytes 196640 | tf_op jit(solution)/shard_map/ppermute | solution.py:19
  176.5 3.7 %collective-permute-start.29 = (bf16[128,768]{1,0:T(8,128)(2,1)S(1)}, bf16[128,768]{1,0:T(8,128)(2,1)S(1)}, u32[]{:S(2)}, u32[]{:S(2)}) collective-permute-start(bf16[128,768]{1,0:T(8,128)(2,1)S(1)} %add_convert_fusion.1), channel_id=1, source_target_pairs={{0,6},{1,7},{2,4},{3,5},{4,2},{5,3},{6,0},{7,1},{8,14},{9,15},{10,... | collective-permute-start | bytes 589832 | tf_op jit(solution)/shard_map/ppermute | solution.py:19
  180.3 2.7 %collective-permute-start.21 = (bf16[128,768]{1,0:T(8,128)(2,1)S(1)}, bf16[128,768]{1,0:T(8,128)(2,1)S(1)}, u32[]{:S(2)}, u32[]{:S(2)}) collective-permute-start(bf16[128,768]{1,0:T(8,128)(2,1)S(1)} %add_convert_fusion.3), channel_id=1, source_target_pairs={{0,8},{1,9},{2,10},{3,11},{4,12},{5,13},{6,14},{7,15},{8,0},{9,1},... | collective-permute-start | bytes 589832 | tf_op jit(solution)/shard_map/ppermute | solution.py:19
  183.0 2.7 %collective-permute-done.29 = bf16[128,768]{1,0:T(8,128)(2,1)S(1)} collective-permute-done((bf16[128,768]{1,0:T(8,128)(2,1)S(1)}, bf16[128,768]{1,0:T(8,128)(2,1)S(1)}, u32[]{:S(2)}, u32[]{:S(2)}) %collective-permute-start.29) | collective-permute-done | bytes 196640 | tf_op jit(solution)/shard_map/ppermute | solution.py:19
  185.7 2.7 %collective-permute-start.30 = (bf16[128,768]{1,0:T(8,128)(2,1)S(1)}, bf16[128,768]{1,0:T(8,128)(2,1)S(1)}, u32[]{:S(2)}, u32[]{:S(2)}) collective-permute-start(bf16[128,768]{1,0:T(8,128)(2,1)S(1)} %add_convert_fusion), channel_id=1, source_target_pairs={{0,8},{1,9},{2,10},{3,11},{4,12},{5,13},{6,14},{7,15},{8,0},{9,1},... | collective-permute-start | bytes 589832 | tf_op jit(solution)/shard_map/ppermute | solution.py:19
  188.5 4.9 %collective-permute-done.30 = bf16[128,768]{1,0:T(8,128)(2,1)S(1)} collective-permute-done((bf16[128,768]{1,0:T(8,128)(2,1)S(1)}, bf16[128,768]{1,0:T(8,128)(2,1)S(1)}, u32[]{:S(2)}, u32[]{:S(2)}) %collective-permute-start.30) | collective-permute-done | bytes 196640 | tf_op jit(solution)/shard_map/ppermute | solution.py:19
  193.5 3.7 %collective-permute-start.31 = (f32[128,1536]{1,0:T(8,128)S(1)}, f32[128,1536]{1,0:T(8,128)S(1)}, u32[]{:S(2)}, u32[]{:S(2)}) collective-permute-start(f32[128,1536]{1,0:T(8,128)S(1)} %pad_maximum_fusion), channel_id=1, source_target_pairs={{0,1},{1,0},{2,3},{3,2},{4,5},{5,4},{6,7},{7,6},{8,9},{9,8},{10,11... | collective-permute-start | bytes 2359304 | tf_op jit(solution)/shard_map/ppermute | solution.py:19
  197.2 12.7 %token_grad.1 = (bf16[1024,1024]{1,0:T(8,128)(2,1)}, bf16[1024,1024]{1,0:T(8,128)(2,1)}) custom-call(s32[42]{0:T(128)S(1)} %concatenate.22.scal_ref, bf16[1024,3072]{1,0:T(8,128)(2,1)} %w_ref.7, bf16[4,1024,128]{2,1,0:T(8,128)(2,1)S(1)} %copy-done.5, bf16[4,1024,128]{2,1,0:T(8,128)(2,1)S(1)} %copy-done.7, bf16[4,512,128]{2,1,0:T(8,128)(2,1)S(1)} %get-tuple-element.30.o1_ref, ...), custom_call_target="tpu_custom_call" | custom-call | flops 6442450944 | bytes 12000000 | tf_op jit(solution)/shard_map/token_grad/pallas_call | solution.py:423
  211.0 1.6 copy.13
  (83 shorter events, 3.7 us)
Async XLA Ops:
  0.6 117.6 %collective-permute-start.11 = (bf16[1024,1024]{1,0:T(8,128)(2,1)}, bf16[1024,1024]{1,0:T(8,128)(2,1)}, u32[]{:S(2)}, u32[]{:S(2)}) collective-permute-start(bf16[1024,1024]{1,0:T(8,128)(2,1)} %bitcast.36), channel_id=1, source_target_pairs={{0,1},{1,0},{2,3},{3,2},{4,5},{5,4},{6,7},{7,6},{8,9},{9,8},{10,11... | collective-permute-start | bytes 6291464 | tf_op jit(solution)/shard_map/ppermute | solution.py:19
  2.9 1.6 copy-start
  4.5 1.6 copy-start.2
  11.2 0.8 copy-start.10
  12.1 45.1 %collective-permute-start = (bf16[4,512,128]{2,1,0:T(8,128)(2,1)}, bf16[4,512,128]{2,1,0:T(8,128)(2,1)S(1)}, u32[]{:S(2)}, u32[]{:S(2)}) collective-permute-start(bf16[4,512,128]{2,1,0:T(8,128)(2,1)} %get-tuple-element.29), channel_id=1, source_target_pairs={{0,16},{16,0},{32,48},{48,32},{64,80},{80,64},{96,112},{112,96},{1... | collective-permute-start | bytes 1572872 | tf_op jit(solution)/shard_map/ppermute | solution.py:19
  21.1 3.8 %copy-start.3 = (bf16[1,1024,1024]{2,1,0:T(8,128)(2,1)S(1)}, bf16[1,1024,1024]{2,1,0:T(8,128)(2,1)}, u32[]{:S(2)}) copy-start(bf16[1,1024,1024]{2,1,0:T(8,128)(2,1)} %param.7) | copy-start | bytes 6291460
  21.1 31.0 %collective-permute-start.2 = (bf16[4,384,128]{2,1,0:T(8,128)(2,1)}, bf16[4,384,128]{2,1,0:T(8,128)(2,1)S(1)}, u32[]{:S(2)}, u32[]{:S(2)}) collective-permute-start(bf16[4,384,128]{2,1,0:T(8,128)(2,1)} %get-tuple-element.33), channel_id=1, source_target_pairs={{0,16},{16,0},{32,48},{48,32},{64,80},{80,64},{96,112},{112,96},{1... | collective-permute-start | bytes 1179656 | tf_op jit(solution)/shard_map/ppermute | solution.py:19
  38.1 50.0 %copy-start.4 = (bf16[4,1024,128]{2,1,0:T(8,128)(2,1)}, bf16[4,1024,128]{2,1,0:T(8,128)(2,1)S(1)}, u32[]{:S(2)}) copy-start(bf16[4,1024,128]{2,1,0:T(8,128)(2,1)S(1)} %attention_dense.2.d0_ref) | copy-start | bytes 3145732
  51.4 36.8 %copy-start.6 = (bf16[4,1024,128]{2,1,0:T(8,128)(2,1)}, bf16[4,1024,128]{2,1,0:T(8,128)(2,1)S(1)}, u32[]{:S(2)}) copy-start(bf16[4,1024,128]{2,1,0:T(8,128)(2,1)S(1)} %attention_dense.3.d1_ref) | copy-start | bytes 3145732
  52.1 23.0 %collective-permute-start.4 = (bf16[2,256,128]{2,1,0:T(8,128)(2,1)S(1)}, bf16[2,256,128]{2,1,0:T(8,128)(2,1)S(1)}, u32[]{:S(2)}, u32[]{:S(2)}) collective-permute-start(bf16[2,256,128]{2,1,0:T(8,128)(2,1)S(1)} %pad_maximum_fusion.4), channel_id=1, source_target_pairs={{0,64},{16,80},{32,96},{48,112},{64,0},{80,16},{96,32},{112,48},{1... | collective-permute-start | bytes 393224 | tf_op jit(solution)/shard_map/ppermute | solution.py:19
  55.0 20.2 %collective-permute-start.5 = (bf16[2,256,128]{2,1,0:T(8,128)(2,1)S(1)}, bf16[2,256,128]{2,1,0:T(8,128)(2,1)S(1)}, u32[]{:S(2)}, u32[]{:S(2)}) collective-permute-start(bf16[2,256,128]{2,1,0:T(8,128)(2,1)S(1)} %pad_maximum_fusion.4), channel_id=1, source_target_pairs={{0,96},{16,112},{32,64},{48,80},{64,32},{80,48},{96,0},{112,16},{1... | collective-permute-start | bytes 393224 | tf_op jit(solution)/shard_map/ppermute | solution.py:19
  56.8 18.4 %collective-permute-start.3 = (bf16[2,768,128]{2,1,0:T(8,128)(2,1)S(1)}, bf16[2,768,128]{2,1,0:T(8,128)(2,1)S(1)}, u32[]{:S(2)}, u32[]{:S(2)}) collective-permute-start(bf16[2,768,128]{2,1,0:T(8,128)(2,1)S(1)} %pad_maximum_fusion.3), channel_id=1, source_target_pairs={{0,32},{16,48},{32,0},{48,16},{64,96},{80,112},{96,64},{112,80},{1... | collective-permute-start | bytes 1179656 | tf_op jit(solution)/shard_map/ppermute | solution.py:19
  57.1 0.8 copy-start.12
  57.9 1.0 copy-start.11
  59.0 1.0 copy-start.13
  74.0 36.2 %collective-permute-start.1 = (bf16[4,512,128]{2,1,0:T(8,128)(2,1)}, bf16[4,512,128]{2,1,0:T(8,128)(2,1)}, u32[]{:S(2)}, u32[]{:S(2)}) collective-permute-start(bf16[4,512,128]{2,1,0:T(8,128)(2,1)} %get-tuple-element.31), channel_id=1, source_target_pairs={{0,16},{16,0},{32,48},{48,32},{64,80},{80,64},{96,112},{112,96},{1... | collective-permute-start | bytes 1572872 | tf_op jit(solution)/shard_map/ppermute | solution.py:19
  85.0 18.3 %collective-permute-start.6 = (bf16[2,768,128]{2,1,0:T(8,128)(2,1)S(1)}, bf16[2,768,128]{2,1,0:T(8,128)(2,1)S(1)}, u32[]{:S(2)}, u32[]{:S(2)}) collective-permute-start(bf16[2,768,128]{2,1,0:T(8,128)(2,1)S(1)} %get-tuple-element.38), channel_id=1, source_target_pairs={{0,32},{16,48},{32,0},{48,16},{64,96},{80,112},{96,64},{112,80},{1... | collective-permute-start | bytes 1179656 | tf_op jit(solution)/shard_map/ppermute | solution.py:19
  86.5 11.8 %collective-permute-start.7 = (bf16[2,256,128]{2,1,0:T(8,128)(2,1)S(1)}, bf16[2,256,128]{2,1,0:T(8,128)(2,1)S(1)}, u32[]{:S(2)}, u32[]{:S(2)}) collective-permute-start(bf16[2,256,128]{2,1,0:T(8,128)(2,1)S(1)} %get-tuple-element.39), channel_id=1, source_target_pairs={{0,64},{16,80},{32,96},{48,112},{64,0},{80,16},{96,32},{112,48},{1... | collective-permute-start | bytes 393224 | tf_op jit(solution)/shard_map/ppermute | solution.py:19
  89.1 16.0 %copy-start.14 = (s32[1,16]{1,0:T(1,128)S(1)}, s32[1,16]{1,0:T(1,128)}, u32[]{:S(2)}) copy-start(s32[1,16]{1,0:T(1,128)} %param.6) | copy-start | bytes 196
  89.1 29.1 %collective-permute-start.12 = (bf16[3,1024,128]{2,1,0:T(8,128)(2,1)}, bf16[3,1024,128]{2,1,0:T(8,128)(2,1)}, u32[]{:S(2)}, u32[]{:S(2)}) collective-permute-start(bf16[3,1024,128]{2,1,0:T(8,128)(2,1)} %get-tuple-element.56), channel_id=1, source_target_pairs={{0,1},{1,0},{2,3},{3,2},{4,5},{5,4},{6,7},{7,6},{8,9},{9,8},{10,11... | collective-permute-start | bytes 2359304 | tf_op jit(solution)/shard_map/ppermute | solution.py:19
  98.3 5.0 %collective-permute-start.8 = (bf16[2,256,128]{2,1,0:T(8,128)(2,1)S(1)}, bf16[2,256,128]{2,1,0:T(8,128)(2,1)S(1)}, u32[]{:S(2)}, u32[]{:S(2)}) collective-permute-start(bf16[2,256,128]{2,1,0:T(8,128)(2,1)S(1)} %get-tuple-element.40), channel_id=1, source_target_pairs={{0,96},{16,112},{32,64},{48,80},{64,32},{80,48},{96,0},{112,16},{1... | collective-permute-start | bytes 393224 | tf_op jit(solution)/shard_map/ppermute | solution.py:19
  104.2 0.8 copy-start.8
  104.9 13.3 %copy-start.1 = (bf16[1,1024,1024]{2,1,0:T(8,128)(2,1)S(1)}, bf16[1,1024,1024]{2,1,0:T(8,128)(2,1)}, u32[]{:S(2)}) copy-start(bf16[1,1024,1024]{2,1,0:T(8,128)(2,1)} %param.4) | copy-start | bytes 6291460
  104.9 6.9 %collective-permute-start.9 = (bf16[4,384,128]{2,1,0:T(8,128)(2,1)}, bf16[4,384,128]{2,1,0:T(8,128)(2,1)}, u32[]{:S(2)}, u32[]{:S(2)}) collective-permute-start(bf16[4,384,128]{2,1,0:T(8,128)(2,1)} %get-tuple-element.42), channel_id=1, source_target_pairs={{0,16},{16,0},{32,48},{48,32},{64,80},{80,64},{96,112},{112,96},{1... | collective-permute-start | bytes 1179656 | tf_op jit(solution)/shard_map/ppermute | solution.py:19
  105.1 5.0 %collective-permute-start.10 = (s32[16]{0:T(128)S(1)}, s32[16]{0:T(128)S(1)}, u32[]{:S(2)}, u32[]{:S(2)}) collective-permute-start(s32[16]{0:T(128)S(1)} %bitcast.53), channel_id=1, source_target_pairs={{0,1},{1,0},{2,3},{3,2},{4,5},{5,4},{6,7},{7,6},{8,9},{9,8},{10,11... | collective-permute-start | bytes 200 | tf_op jit(solution)/shard_map/ppermute | solution.py:19
  111.3 12.9 %collective-permute-start.15 = (bf16[3,512,128]{2,1,0:T(8,128)(2,1)S(1)}, bf16[3,512,128]{2,1,0:T(8,128)(2,1)S(1)}, u32[]{:S(2)}, u32[]{:S(2)}) collective-permute-start(bf16[3,512,128]{2,1,0:T(8,128)(2,1)S(1)} %get-tuple-element.60), channel_id=1, source_target_pairs={{0,1},{1,0},{2,3},{3,2},{4,5},{5,4},{6,7},{7,6},{8,9},{9,8},{10,11... | collective-permute-start | bytes 1179656 | tf_op jit(solution)/shard_map/ppermute | solution.py:19
  113.0 17.8 %collective-permute-start.22 = (bf16[3,384,128]{2,1,0:T(8,128)(2,1)S(1)}, bf16[3,384,128]{2,1,0:T(8,128)(2,1)S(1)}, u32[]{:S(2)}, u32[]{:S(2)}) collective-permute-start(bf16[3,384,128]{2,1,0:T(8,128)(2,1)S(1)} %get-tuple-element.62), channel_id=1, source_target_pairs={{0,1},{1,0},{2,3},{3,2},{4,5},{5,4},{6,7},{7,6},{8,9},{9,8},{10,11... | collective-permute-start | bytes 884744 | tf_op jit(solution)/shard_map/ppermute | solution.py:19
  124.1 20.4 %collective-permute-start.13 = (bf16[2,256,384]{2,1,0:T(8,128)(2,1)S(1)}, bf16[2,256,384]{2,1,0:T(8,128)(2,1)S(1)}, u32[]{:S(2)}, u32[]{:S(2)}) collective-permute-start(bf16[2,256,384]{2,1,0:T(8,128)(2,1)S(1)} %get-tuple-element.46), channel_id=1, source_target_pairs={{0,32},{16,48},{32,0},{48,16},{64,96},{80,112},{96,64},{112,80},{1... | collective-permute-start | bytes 1179656 | tf_op jit(solution)/shard_map/ppermute | solution.py:19
  129.8 15.9 %collective-permute-start.16 = (bf16[2,256,384]{2,1,0:T(8,128)(2,1)S(1)}, bf16[2,256,384]{2,1,0:T(8,128)(2,1)S(1)}, u32[]{:S(2)}, u32[]{:S(2)}) collective-permute-start(bf16[2,256,384]{2,1,0:T(8,128)(2,1)S(1)} %get-tuple-element.48), channel_id=1, source_target_pairs={{0,96},{16,112},{32,64},{48,80},{64,32},{80,48},{96,0},{112,16},{1... | collective-permute-start | bytes 1179656 | tf_op jit(solution)/shard_map/ppermute | solution.py:19
  136.2 10.5 %collective-permute-start.23 = (bf16[2,256,384]{2,1,0:T(8,128)(2,1)S(1)}, bf16[2,256,384]{2,1,0:T(8,128)(2,1)S(1)}, u32[]{:S(2)}, u32[]{:S(2)}) collective-permute-start(bf16[2,256,384]{2,1,0:T(8,128)(2,1)S(1)} %get-tuple-element.50), channel_id=1, source_target_pairs={{0,32},{16,48},{32,0},{48,16},{64,96},{80,112},{96,64},{112,80},{1... | collective-permute-start | bytes 1179656 | tf_op jit(solution)/shard_map/ppermute | solution.py:19
  142.7 11.1 %collective-permute-start.25 = (bf16[2,256,384]{2,1,0:T(8,128)(2,1)S(1)}, bf16[2,256,384]{2,1,0:T(8,128)(2,1)S(1)}, u32[]{:S(2)}, u32[]{:S(2)}) collective-permute-start(bf16[2,256,384]{2,1,0:T(8,128)(2,1)S(1)} %get-tuple-element.52), channel_id=1, source_target_pairs={{0,96},{16,112},{32,64},{48,80},{64,32},{80,48},{96,0},{112,16},{1... | collective-permute-start | bytes 1179656 | tf_op jit(solution)/shard_map/ppermute | solution.py:19
  144.7 13.3 %collective-permute-start.14 = (bf16[256,384]{1,0:T(8,128)(2,1)S(1)}, bf16[256,384]{1,0:T(8,128)(2,1)S(1)}, u32[]{:S(2)}, u32[]{:S(2)}) collective-permute-start(bf16[256,384]{1,0:T(8,128)(2,1)S(1)} %fusion.2), channel_id=1, source_target_pairs={{0,96},{16,112},{32,64},{48,80},{64,32},{80,48},{96,0},{112,16},{1... | collective-permute-start | bytes 589832 | tf_op jit(solution)/shard_map/ppermute | solution.py:19
  145.7 12.2 %collective-permute-start.17 = (bf16[256,384]{1,0:T(8,128)(2,1)S(1)}, bf16[256,384]{1,0:T(8,128)(2,1)S(1)}, u32[]{:S(2)}, u32[]{:S(2)}) collective-permute-start(bf16[256,384]{1,0:T(8,128)(2,1)S(1)} %fusion.3), channel_id=1, source_target_pairs={{0,32},{16,48},{32,0},{48,16},{64,96},{80,112},{96,64},{112,80},{1... | collective-permute-start | bytes 589832 | tf_op jit(solution)/shard_map/ppermute | solution.py:19
  146.8 15.3 %collective-permute-start.24 = (bf16[256,384]{1,0:T(8,128)(2,1)S(1)}, bf16[256,384]{1,0:T(8,128)(2,1)S(1)}, u32[]{:S(2)}, u32[]{:S(2)}) collective-permute-start(bf16[256,384]{1,0:T(8,128)(2,1)S(1)} %fusion.4), channel_id=1, source_target_pairs={{0,96},{16,112},{32,64},{48,80},{64,32},{80,48},{96,0},{112,16},{1... | collective-permute-start | bytes 589832 | tf_op jit(solution)/shard_map/ppermute | solution.py:19
  153.8 8.4 %collective-permute-start.26 = (bf16[256,384]{1,0:T(8,128)(2,1)S(1)}, bf16[256,384]{1,0:T(8,128)(2,1)S(1)}, u32[]{:S(2)}, u32[]{:S(2)}) collective-permute-start(bf16[256,384]{1,0:T(8,128)(2,1)S(1)} %fusion.5), channel_id=1, source_target_pairs={{0,32},{16,48},{32,0},{48,16},{64,96},{80,112},{96,64},{112,80},{1... | collective-permute-start | bytes 589832 | tf_op jit(solution)/shard_map/ppermute | solution.py:19
  158.1 4.9 %collective-permute-start.18 = (bf16[128,768]{1,0:T(8,128)(2,1)S(1)}, bf16[128,768]{1,0:T(8,128)(2,1)S(1)}, u32[]{:S(2)}, u32[]{:S(2)}) collective-permute-start(bf16[128,768]{1,0:T(8,128)(2,1)S(1)} %select_convert_fusion.3), channel_id=1, source_target_pairs={{0,16},{16,0},{32,48},{48,32},{64,80},{80,64},{96,112},{112,96},{1... | collective-permute-start | bytes 589832 | tf_op jit(solution)/shard_map/ppermute | solution.py:19
  162.3 6.9 %collective-permute-start.27 = (bf16[128,768]{1,0:T(8,128)(2,1)S(1)}, bf16[128,768]{1,0:T(8,128)(2,1)S(1)}, u32[]{:S(2)}, u32[]{:S(2)}) collective-permute-start(bf16[128,768]{1,0:T(8,128)(2,1)S(1)} %select_convert_fusion), channel_id=1, source_target_pairs={{0,16},{16,0},{32,48},{48,32},{64,80},{80,64},{96,112},{112,96},{1... | collective-permute-start | bytes 589832 | tf_op jit(solution)/shard_map/ppermute | solution.py:19
  163.0 8.0 %collective-permute-start.19 = (bf16[128,768]{1,0:T(8,128)(2,1)S(1)}, bf16[128,768]{1,0:T(8,128)(2,1)S(1)}, u32[]{:S(2)}, u32[]{:S(2)}) collective-permute-start(bf16[128,768]{1,0:T(8,128)(2,1)S(1)} %add_convert_fusion.5), channel_id=1, source_target_pairs={{0,2},{1,3},{2,0},{3,1},{4,6},{5,7},{6,4},{7,5},{8,10},{9,11},{10,... | collective-permute-start | bytes 589832 | tf_op jit(solution)/shard_map/ppermute | solution.py:19
  169.3 7.1 %collective-permute-start.28 = (bf16[128,768]{1,0:T(8,128)(2,1)S(1)}, bf16[128,768]{1,0:T(8,128)(2,1)S(1)}, u32[]{:S(2)}, u32[]{:S(2)}) collective-permute-start(bf16[128,768]{1,0:T(8,128)(2,1)S(1)} %add_convert_fusion.2), channel_id=1, source_target_pairs={{0,2},{1,3},{2,0},{3,1},{4,6},{5,7},{6,4},{7,5},{8,10},{9,11},{10,... | collective-permute-start | bytes 589832 | tf_op jit(solution)/shard_map/ppermute | solution.py:19
  171.1 9.1 %collective-permute-start.20 = (bf16[128,768]{1,0:T(8,128)(2,1)S(1)}, bf16[128,768]{1,0:T(8,128)(2,1)S(1)}, u32[]{:S(2)}, u32[]{:S(2)}) collective-permute-start(bf16[128,768]{1,0:T(8,128)(2,1)S(1)} %add_convert_fusion.4), channel_id=1, source_target_pairs={{0,6},{1,7},{2,4},{3,5},{4,2},{5,3},{6,0},{7,1},{8,14},{9,15},{10,... | collective-permute-start | bytes 589832 | tf_op jit(solution)/shard_map/ppermute | solution.py:19
  176.5 9.2 %collective-permute-start.29 = (bf16[128,768]{1,0:T(8,128)(2,1)S(1)}, bf16[128,768]{1,0:T(8,128)(2,1)S(1)}, u32[]{:S(2)}, u32[]{:S(2)}) collective-permute-start(bf16[128,768]{1,0:T(8,128)(2,1)S(1)} %add_convert_fusion.1), channel_id=1, source_target_pairs={{0,6},{1,7},{2,4},{3,5},{4,2},{5,3},{6,0},{7,1},{8,14},{9,15},{10,... | collective-permute-start | bytes 589832 | tf_op jit(solution)/shard_map/ppermute | solution.py:19
  180.3 8.2 %collective-permute-start.21 = (bf16[128,768]{1,0:T(8,128)(2,1)S(1)}, bf16[128,768]{1,0:T(8,128)(2,1)S(1)}, u32[]{:S(2)}, u32[]{:S(2)}) collective-permute-start(bf16[128,768]{1,0:T(8,128)(2,1)S(1)} %add_convert_fusion.3), channel_id=1, source_target_pairs={{0,8},{1,9},{2,10},{3,11},{4,12},{5,13},{6,14},{7,15},{8,0},{9,1},... | collective-permute-start | bytes 589832 | tf_op jit(solution)/shard_map/ppermute | solution.py:19
  185.7 11.5 %copy-start.5 = (bf16[4,1024,128]{2,1,0:T(8,128)(2,1)S(1)}, bf16[4,1024,128]{2,1,0:T(8,128)(2,1)}, u32[]{:S(2)}) copy-start(bf16[4,1024,128]{2,1,0:T(8,128)(2,1)} %copy-done.4) | copy-start | bytes 3145732
  185.7 11.5 %copy-start.7 = (bf16[4,1024,128]{2,1,0:T(8,128)(2,1)S(1)}, bf16[4,1024,128]{2,1,0:T(8,128)(2,1)}, u32[]{:S(2)}) copy-start(bf16[4,1024,128]{2,1,0:T(8,128)(2,1)} %copy-done.6) | copy-start | bytes 3145732
  185.7 11.5 %copy-start.9 = (bf16[4,384,128]{2,1,0:T(8,128)(2,1)S(1)}, bf16[4,384,128]{2,1,0:T(8,128)(2,1)}, u32[]{:S(2)}) copy-start(bf16[4,384,128]{2,1,0:T(8,128)(2,1)} %copy-done.8) | copy-start | bytes 1179652
  185.7 7.7 %collective-permute-start.30 = (bf16[128,768]{1,0:T(8,128)(2,1)S(1)}, bf16[128,768]{1,0:T(8,128)(2,1)S(1)}, u32[]{:S(2)}, u32[]{:S(2)}) collective-permute-start(bf16[128,768]{1,0:T(8,128)(2,1)S(1)} %add_convert_fusion), channel_id=1, source_target_pairs={{0,8},{1,9},{2,10},{3,11},{4,12},{5,13},{6,14},{7,15},{8,0},{9,1},... | collective-permute-start | bytes 589832 | tf_op jit(solution)/shard_map/ppermute | solution.py:19
  193.5 16.4 %collective-permute-start.31 = (f32[128,1536]{1,0:T(8,128)S(1)}, f32[128,1536]{1,0:T(8,128)S(1)}, u32[]{:S(2)}, u32[]{:S(2)}) collective-permute-start(f32[128,1536]{1,0:T(8,128)S(1)} %pad_maximum_fusion), channel_id=1, source_target_pairs={{0,1},{1,0},{2,3},{3,2},{4,5},{5,4},{6,7},{7,6},{8,9},{9,8},{10,11... | collective-permute-start | bytes 2359304 | tf_op jit(solution)/shard_map/ppermute | solution.py:19
